TPU v7x, 32 devices: a whole 2x2x4 slice. The times are simulated.
32 devices in a mesh: groups: 2 (over x), dom: 16 (over z, y, core).
Axes of the slice: x: 2, y: 2, z: 4, core: 2. Of those that a mesh axis runs over, the one named last changes fastest.
Arguments:
- source: bfloat16 [72, 262144], P(None, ('groups', 'dom')), parts along dimension 1, may hold values from -6 to 6
- tile_weight: bfloat16 [8192, 128, 128], P('dom'), may hold values from -0.0625 to 0.0625
- tile_source: int32 [8192], P('dom'), may hold values from 0 to 127
- tile_slot: int32 [8192], P('dom'), may hold values from 0 to 15
- tile_count: int32 [16], P('dom'), may hold values from 64 to 512, as said below
- dest_block: int32 [256], P('dom'), may hold values from 0 to 63, as said below
- embed_weight: bfloat16 [1152, 1024], replicated, may hold values from -0.1875 to 0.1875
- embed_bias: float32 [1024], replicated, may hold values from -3 to 3
Outputs:
- remapped: bfloat16 [128, 72, 128], P(('groups', 'dom')), parts along dimension 0
- embedded: bfloat16 [1024, 1024], P(('groups', 'dom')), parts along dimension 0
There are 2 independent parts, one for each index of `groups`. A program takes and returns all parts, laid end to end along the dimension named above; an argument that names none is the same for every part. Nothing has to cross between parts.
Inputs may be any that keep to these rules, and one draw needn't show every extreme that they name: `tile_count`: number of live tiles of each device; the later tile slots are unused. Some device has all 512 tiles live. `dest_block`: the owner of target block b is device b // 4. Within one device's 16 entries the blocks are distinct and at most 2 of them belong to any one owner; on every device some owner has exactly 2.
All inputs are finite; a program needn't handle non-finite values.
Results may differ from a plain program's by a relative error of at most 0.0046.
Values may be sent and summed in bfloat16 or wider, within the bound.
No kernel may reach another device: no remote copies, remote signals or barrier semaphores. Data moves between devices by JAX's collectives and lax.ppermute only.
A program may use at most 128 MiB of HBM per device.

v0:
```python
import functools

import jax
import jax.numpy as jnp
from jax import lax
from jax.experimental import pallas as pl
from jax.experimental.pallas import tpu as pltpu
from jax.sharding import PartitionSpec as P

PATCH = 4
CAP = 2
TB_DEV = 4
LANES = 128
SEG = 4
EARLY_UNROLL = 16
LATE_UNROLL = 8
CHUNK = 64
VMEM = pl.BlockSpec(memory_space=pltpu.VMEM)
SMEM = pl.BlockSpec(memory_space=pltpu.SMEM)
ANY = pl.BlockSpec(memory_space=pl.ANY)


def list_rows(tiles, slots):
    step = SEG * EARLY_UNROLL
    entries = -(-(-(-(tiles + slots * (SEG - 1)) // step) * step) // LANES)
    segments = -(-entries // SEG)
    return entries, segments, -(-(2 * (entries + segments) + 1) // 8) * 8


def iota(shape, dim):
    return lax.broadcasted_iota(jnp.int32, shape, dim)


def schedule(source, slot, live, core, slots, own, rim, out):
    tiles = source.shape[1]
    bits = tiles.bit_length()
    entries, segments, rows = list_rows(tiles, slots)
    ids = iota((1, tiles), 1)
    on_left, on_right = source < rim, source >= rim + own
    inner = ~(on_left | on_right)
    near = (on_left & (core == 1)) | (on_right & (core == 0))
    offset = jnp.where(on_right, source - own - rim, source)
    block = jnp.where(inner, source - rim, jnp.where(near, own + offset, offset))
    late = ~(inner | near)
    bins = jnp.where(ids < live, slot + jnp.where(late, slots, 0), -1)
    chosen = bins == iota((2 * slots, tiles), 0)
    ones = jnp.where(chosen, 1.0, 0.0)
    before = jnp.where(iota((tiles, tiles), 0) < iota((tiles, tiles), 1), 1.0, 0.0)
    rank = jnp.dot(
        ones.astype(jnp.bfloat16), before.astype(jnp.bfloat16), preferred_element_type=jnp.float32
    )
    total = jnp.sum(ones, axis=1, keepdims=True).astype(jnp.int32)
    length = jnp.broadcast_to((total + (SEG - 1)) // SEG, (2 * slots, LANES))
    a, b = iota((2 * slots, 2 * slots), 0), iota((2 * slots, 2 * slots), 1)
    upto = jnp.where((b <= a) & ((b >= slots) == (a >= slots)), 1.0, 0.0)
    ends = jnp.dot(
        upto.astype(jnp.bfloat16),
        length.astype(jnp.float32).astype(jnp.bfloat16),
        preferred_element_type=jnp.float32,
    ).astype(jnp.int32)
    begins = (ends - length)[:, :1].astype(jnp.float32)
    place = jnp.sum(jnp.where(chosen, rank + begins * SEG, 0.0), axis=0, keepdims=True)
    place = place.astype(jnp.int32) + jnp.where(late, entries * LANES, 0)
    place = jnp.where(bins >= 0, place, -1)
    count = tiles - ids
    at_row = (place >> 7) == iota((rows, tiles), 0)
    at_lane = jnp.where((place & (LANES - 1)) == iota((LANES, tiles), 0), 1.0, 0.0)

    def listed(value):
        return lax.dot_general(
            jnp.where(at_row, value.astype(jnp.float32), 0.0).astype(jnp.bfloat16),
            at_lane.astype(jnp.bfloat16),
            (((1,), (1,)), ((), ())),
            preferred_element_type=jnp.float32,
        ).astype(jnp.int32)

    out[...] = (listed(block) << bits) | (listed(count >> 5) << 5) | listed(count & 31)
    for k in range(2):
        mine = ends[k * slots : (k + 1) * slots, :]
        for r in range(segments):
            passed = jnp.where(mine <= iota((slots, LANES), 1) + r * LANES, 1.0, 0.0)
            owner = jnp.sum(passed, axis=0, keepdims=True).astype(jnp.int32)
            spot = 2 * entries + k * segments + r
            out[spot : spot + 1, :] = jnp.minimum(owner, slots - 1)
    spot = 2 * (entries + segments)
    out[spot : spot + 1, :] = jnp.where(
        iota((1, LANES), 1) == 0, ends[slots - 1 : slots, :], ends[2 * slots - 1 : 2 * slots, :]
    )


def run_segments(kind, unroll, tiles, slots, meta, x, w, acc):
    entries, segments, _ = list_rows(tiles, slots)
    bits = tiles.bit_length()
    total = meta[2 * (entries + segments), kind]

    def step(i, carry):
        results = []
        for u in range(unroll):
            first = (i * unroll + u) * SEG
            row, lane = kind * entries + (first >> 7), first & (LANES - 1)
            xs, ws = [], []
            for k in range(SEG):
                code = meta[row, lane + k]
                column = pl.multiple_of((code >> bits) * LANES, LANES)
                xs.append(x[:, pl.ds(column, LANES)])
                ws.append(w[tiles - (code & ((1 << bits) - 1))])
            results.append(
                jnp.dot(
                    jnp.concatenate(xs, axis=1),
                    jnp.concatenate(ws, axis=0),
                    preferred_element_type=jnp.float32,
                )
            )
        for u in range(unroll):
            g = i * unroll + u
            slot = meta[2 * entries + kind * segments + (g >> 7), g & (LANES - 1)]
            acc[slot] += results[u]
        return carry

    lax.fori_loop(0, (total + unroll - 1) // unroll, step, 0)


def early_kernel(
    slots, core, count, tile_source, tile_slot, source, near, weights, acc, held, lists, x, ids, meta, sems
):
    tiles = tile_source.shape[1]
    cells = source.shape[1]
    live = count[0]
    chunks = tiles // CHUNK

    def copy(c):
        part = pl.ds(c * CHUNK, CHUNK)
        return pltpu.make_async_copy(weights.at[part], held.at[part], sems.at[c])

    ids_in = [
        pltpu.make_async_copy(tile_source, ids.at[0], sems.at[chunks + 3]),
        pltpu.make_async_copy(tile_slot, ids.at[1], sems.at[chunks + 4]),
    ]
    for c in ids_in:
        c.start()
    for c in range(chunks):
        pl.when(c * CHUNK < live)(lambda c=c: copy(c).start())
    half = cells // 2
    first = pl.multiple_of(core[0] * half, LANES)
    cells_in = [
        pltpu.make_async_copy(source, x.at[:, pl.ds(0, cells)], sems.at[chunks]),
        pltpu.make_async_copy(
            near.at[:, pl.ds(first, half)], x.at[:, pl.ds(cells, half)], sems.at[chunks + 1]
        ),
    ]
    for c in cells_in:
        c.start()
    own = cells // LANES
    for c in ids_in:
        c.wait()
    schedule(ids[0], ids[1], live, core[0], slots, own, own // 2, lists)
    to_scalars = pltpu.make_async_copy(lists, meta, sems.at[chunks + 2])
    to_scalars.start()
    acc[...] = jnp.zeros_like(acc)
    held[tiles] = jnp.zeros(held.shape[1:], held.dtype)
    to_scalars.wait()
    for c in cells_in:
        c.wait()
    for c in range(chunks):
        pl.when(c * CHUNK < live)(lambda c=c: copy(c).wait())
    run_segments(0, EARLY_UNROLL, tiles, slots, meta, x, held, acc)


def late_kernel(tiles, slots, meta, place, far, partial, held, *rest):
    *outs, acc = rest
    acc[...] = partial[...]
    for out in outs:
        out[...] = jnp.zeros_like(out)
    run_segments(1, LATE_UNROLL, tiles, slots, meta, far, held, acc)

    def put(s, carry):
        code = place[s]
        for q, out in enumerate(outs):

            @pl.when((code >> 16) == q)
            def _(out=out):
                out[code & 0xFFFF] = acc[s].astype(out.dtype)

        return carry

    lax.fori_loop(0, slots, put, 0)


def plane_kernel(planes, me, *refs):
    members = len([r for r in refs if len(r.shape) == 1]) + 1
    labels, (own, *rows), rest = refs[: members - 1], refs[members - 1 : 2 * members - 1], refs[2 * members - 1 :]
    *outs, total = rest
    total[...] = own[...]
    for label, row in zip(labels, rows):
        for r in range(row.shape[0]):
            spot = label[r]

            @pl.when(spot >= 0)
            def _(r=r, row=row, spot=spot):
                total[(r // CAP) * TB_DEV + spot] += row[r].astype(jnp.float32)

    if len(outs) == 1:
        outs[0][...] = total[...].astype(outs[0].dtype)
    else:
        for m, out in enumerate(outs):
            out[...] = total[pl.ds((me[0] ^ m) * TB_DEV, TB_DEV)].astype(out.dtype)


def final_kernel(choose, weight, bias, *refs):
    *parts, remapped, embedded, turned = refs
    blocks, channels, cells = remapped.shape
    for b in range(blocks):
        value = sum(p[i + b].astype(jnp.float32) for p in parts for i in range(0, p.shape[0], blocks))
        value = value.astype(jnp.bfloat16)
        remapped[b] = value
        turned[b] = lax.dot_general(
            choose[...], value, (((1,), (1,)), ((), ())), preferred_element_type=jnp.float32
        )
    per_block = cells // (PATCH * PATCH)
    total = jnp.broadcast_to(bias[...], (blocks * per_block, bias.shape[1]))
    for s in range(PATCH * PATCH):
        rows = turned[:, s * per_block : (s + 1) * per_block, :]
        rows = rows.reshape(blocks * per_block, channels).astype(jnp.bfloat16)
        total = total + jnp.dot(rows, weight[s], preferred_element_type=jnp.float32)
    embedded[...] = total.astype(jnp.bfloat16)


def chooser(cells):
    per_block = cells // (PATCH * PATCH)
    row = jnp.arange(cells, dtype=jnp.int32)
    r, q, p = row // (PATCH * per_block), row // per_block % PATCH, row % per_block
    wanted = r * (PATCH * per_block) + p * PATCH + q
    return (wanted[:, None] == jnp.arange(cells, dtype=jnp.int32)[None, :]).astype(jnp.bfloat16)


def in_vmem(x):
    return pltpu.with_memory_space_constraint(x, pltpu.VMEM)


def in_hbm(x):
    return pltpu.with_memory_space_constraint(x, pltpu.HBM)


def limit(mib):
    return pltpu.CompilerParams(vmem_limit_bytes=mib << 20)


def local(
    source, tile_weight, tile_source, tile_slot, tile_count, dest_block, embed_weight, embed_bias
):
    channels, own_cells = source.shape
    tiles, block_size, _ = tile_weight.shape
    slots = dest_block.shape[0]
    peers = lax.axis_size("dom")
    me = lax.axis_index("dom").astype(jnp.int32)
    core = me & 1
    width = own_cells // 2
    emb = embed_weight.shape[1]
    members = 4 if peers == 16 else 2
    planes = peers // members

    def swap(x, q):
        return lax.ppermute(x, "dom", [(i, i ^ q) for i in range(peers)])

    near = swap(source, 1)
    far = lax.ppermute(
        lax.dynamic_slice_in_dim(source, core * width, width, axis=1),
        "dom",
        [(i, (i + (1 if i % 2 else -1)) % peers) for i in range(peers)],
    )

    acc_shape = (slots, channels, block_size)
    _, _, list_total = list_rows(tiles, slots)
    partial, held, lists = pl.pallas_call(
        functools.partial(early_kernel, slots),
        out_shape=(
            pltpu.VMEM(acc_shape, jnp.float32),
            pltpu.VMEM((tiles + 1, block_size, block_size), jnp.bfloat16),
            jax.ShapeDtypeStruct((list_total, LANES), jnp.int32),
        ),
        in_specs=[SMEM, SMEM, ANY, ANY, ANY, ANY, ANY],
        out_specs=(VMEM, VMEM, VMEM),
        scratch_shapes=[
            pltpu.VMEM((channels, own_cells + width), jnp.bfloat16),
            pltpu.VMEM((2, 1, tiles), jnp.int32),
            pltpu.SMEM((list_total, LANES), jnp.int32),
            pltpu.SemaphoreType.DMA((tiles // CHUNK + 5,)),
        ],
        compiler_params=limit(12),
        cost_estimate=pl.CostEstimate(
            flops=tiles * channels * block_size * block_size,
            bytes_accessed=tile_weight.size * 2,
            transcendentals=0,
        ),
        name="early_tiles",
    )(
        core[None],
        tile_count,
        in_hbm(tile_source[None, :]),
        in_hbm(tile_slot[None, :]),
        in_hbm(source),
        near,
        in_hbm(tile_weight),
    )

    lists, dest_block, embed_weight = lax.optimization_barrier((lists, dest_block, embed_weight))
    slot_ids = jnp.arange(slots, dtype=jnp.int32)
    owners = dest_block // TB_DEV
    earlier = (owners[None, :] == owners[:, None]) & (slot_ids[None, :] < slot_ids[:, None])
    row = owners // members * CAP + jnp.sum(earlier.astype(jnp.int32), axis=1)
    member = (owners % members) ^ (me & (members - 1))
    block_row = dest_block % TB_DEV
    place = jnp.where(member == 0, owners // members * TB_DEV + block_row, (member << 16) | row)
    row_total = planes * CAP
    spots = jnp.arange(members * row_total, dtype=jnp.int32)
    taken = (member * row_total + row)[None, :] == spots[:, None]
    labels = jnp.sum(jnp.where(taken, block_row[None, :] + 1, 0), axis=1) - 1
    labels = [swap(labels[q * row_total : (q + 1) * row_total], q) for q in range(1, members)]
    area = PATCH * PATCH
    weight = embed_weight.reshape(channels, area, emb).transpose(1, 0, 2)
    lists, place, weight, *labels = lax.optimization_barrier((lists, place, weight, *labels))

    own_shape = pltpu.VMEM((planes * TB_DEV, channels, block_size), jnp.float32)
    row_shape = jax.ShapeDtypeStruct((row_total, channels, block_size), jnp.bfloat16)
    own, *rows = pl.pallas_call(
        functools.partial(late_kernel, tiles, slots),
        out_shape=(own_shape,) + (row_shape,) * (members - 1),
        in_specs=[SMEM, SMEM, VMEM, VMEM, VMEM],
        out_specs=(VMEM,) * members,
        scratch_shapes=[pltpu.VMEM(acc_shape, jnp.float32)],
        compiler_params=limit(12),
        cost_estimate=pl.CostEstimate(
            flops=tiles * channels * block_size * block_size,
            bytes_accessed=2 * channels * width * 2,
            transcendentals=0,
        ),
        name="late_tiles",
    )(lists, place, far, in_vmem(partial), in_vmem(held))

    rows = [swap(r, q + 1) for q, r in enumerate(rows)]
    part = (TB_DEV, channels, block_size)
    by_swap = planes <= 4
    if by_swap:
        part_shapes = (pltpu.VMEM(part, jnp.float32),)
        part_shapes += (jax.ShapeDtypeStruct(part, jnp.bfloat16),) * (planes - 1)
    else:
        part_shapes = (jax.ShapeDtypeStruct((planes * TB_DEV,) + part[1:], jnp.bfloat16),)
    parts = pl.pallas_call(
        functools.partial(plane_kernel, planes),
        out_shape=part_shapes,
        in_specs=[SMEM] * members + [VMEM] * members,
        out_specs=(VMEM,) * len(part_shapes),
        scratch_shapes=[pltpu.VMEM(own_shape.shape, jnp.float32)],
        compiler_params=limit(24),
        name="plane_sum",
    )((me // members)[None], *labels, in_vmem(own), *rows)
    if by_swap:
        parts = [parts[0]] + [swap(p, (m + 1) * members) for m, p in enumerate(parts[1:])]
    else:
        columns = [[z * members + i for z in range(planes)] for i in range(members)]
        parts = [lax.all_to_all(parts[0], "dom", 0, 0, tiled=True, axis_index_groups=columns)]

    per_block = block_size // area
    return pl.pallas_call(
        final_kernel,
        out_shape=(
            jax.ShapeDtypeStruct(part, jnp.bfloat16),
            jax.ShapeDtypeStruct((TB_DEV * per_block, emb), jnp.bfloat16),
        ),
        in_specs=[VMEM] * (3 + len(parts)),
        out_specs=(VMEM, VMEM),
        scratch_shapes=[pltpu.VMEM((TB_DEV, block_size, channels), jnp.float32)],
        compiler_params=limit(16),
        name="embed",
    )(chooser(block_size), weight, embed_bias.reshape(1, emb), *parts)


def solution(mesh):
    placed = (
        P(None, ("groups", "dom")),
        P("dom", None, None),
        P("dom"),
        P("dom"),
        P("dom"),
        P("dom"),
        P(),
        P(),
    )
    return jax.shard_map(
        local,
        mesh=mesh,
        in_specs=placed,
        out_specs=(P(("groups", "dom"), None, None), P(("groups", "dom"), None)),
        check_vma=False,
    )
```

profile of v0, /device:TPU:0, one launch (start us, length us, event | category | flops | bytes accessed | tf_op | source)
XLA Modules:
  0.0 47.1 jit_solution(4662246786417885285)
XLA Ops:
  0.6 0.5 %collective-permute-start = (bf16[72,8192]{1,0:T(8,128)(2,1)}, bf16[72,8192]{1,0:T(8,128)(2,1)S(1)}, u32[]{:S(2)}, u32[]{:S(2)}) collective-permute-start(bf16[72,8192]{1,0:T(8,128)(2,1)} %source.1), channel_id=1, source_target_pairs={{0,1},{1,0},{2,3},{3,2},{4,5},{5,4},{6,7},{7,6},{8,9},{9,8},{10,11... | collective-permute-start | bytes 3538952 | tf_op jit(solution)/shard_map/ppermute | solution.py:263
  1.1 1.1 %constant_dynamic-slice_fusion = bf16[72,4096]{1,0:T(8,128)(2,1)S(1)} fusion(bf16[72,8192]{1,0:T(8,128)(2,1)} %source.1, s32[]{:T(128)S(6)} %select_n.79), kind=kLoop, calls=%fused_computation.40 | loop fusion | bytes 1179652 | tf_op jit(solution)/shard_map/dynamic_slice | solution.py:267
  2.3 5.7 %collective-permute-start.4 = (bf16[72,4096]{1,0:T(8,128)(2,1)S(1)}, bf16[72,4096]{1,0:T(8,128)(2,1)S(1)}, u32[]{:S(2)}, u32[]{:S(2)}) collective-permute-start(bf16[72,4096]{1,0:T(8,128)(2,1)S(1)} %constant_dynamic-slice_fusion), channel_id=1, source_target_pairs={{0,15},{1,2},{2,1},{3,4},{4,3},{5,6},{6,5},{7,8},{8,7},{9,10},{10,... | collective-permute-start | bytes 1769480 | tf_op jit(solution)/shard_map/ppermute | solution.py:266
  8.6 0.0 collective-permute-done.near
  8.6 0.0 copy-start.2
  8.7 0.0 copy-start.1
  8.7 2.9 %early_tiles.1 = (f32[16,72,128]{2,1,0:T(8,128)S(1)}, bf16[513,128,128]{2,1,0:T(8,128)(2,1)S(1)}, s32[16,128]{1,0:T(8,128)S(1)}) custom-call(s32[1]{0:T(128)} %bitcast.core, s32[1]{0:T(128)S(6)} %copy.14.count, s32[1,512]{1,0:T(1,128)} %bitcast.12, s32[1,512]{1,0:T(1,128)} %bitcast.13, bf16[72,8192]{1,0:T(8,128)(2,1)} %source.1, ...), custom_call_target="tpu_custom_call" | custom-call | flops 603979776 | bytes 16777216 | tf_op jit(solution)/shard_map/early_tiles/pallas_call | solution.py:274
  11.6 0.2 convert_reduce_fusion
  11.8 0.1 select_reduce_fusion
  11.9 0.1 fusion.9
  12.0 0.0 collective-permute-start.1
  12.0 2.1 %collective-permute-start.2 = (s32[8]{0:T(128)S(1)}, s32[8]{0:T(128)S(1)}, u32[]{:S(2)}, u32[]{:S(2)}) collective-permute-start(s32[8]{0:T(128)S(1)} %get-tuple-element.48), channel_id=1, source_target_pairs={{0,2},{1,3},{2,0},{3,1},{4,6},{5,7},{6,4},{7,5},{8,10},{9,11},{10,... | collective-permute-start | bytes 104 | tf_op jit(solution)/shard_map/ppermute | solution.py:263
  14.1 0.0 collective-permute-start.3
  14.1 1.3 %copy.13 = bf16[72,16,1024]{2,0,1:T(8,128)(2,1)S(1)} copy(bf16[72,16,1024]{2,1,0:T(8,128)(2,1)S(1)} %bitcast.11) | data formatting | bytes 4718592 | tf_op jit(solution)/shard_map/reshape | solution.py:320
  15.4 0.0 collective-permute-done.1.refs_0_
  15.4 3.6 %collective-permute-done.2.refs_1_ = s32[8]{0:T(128)S(1)} collective-permute-done((s32[8]{0:T(128)S(1)}, s32[8]{0:T(128)S(1)}, u32[]{:S(2)}, u32[]{:S(2)}) %collective-permute-start.2) | collective-permute-done | bytes 64 | tf_op jit(solution)/shard_map/ppermute | solution.py:263
  19.0 0.0 collective-permute-done.3.refs_2_
  19.0 0.0 collective-permute-done.4.far
  19.0 2.8 %late_tiles.1 = (f32[16,72,128]{2,1,0:T(8,128)S(1)}, bf16[8,72,128]{2,1,0:T(8,128)(2,1)}, bf16[8,72,128]{2,1,0:T(8,128)(2,1)}, bf16[8,72,128]{2,1,0:T(8,128)(2,1)}) custom-call(s32[16,128]{1,0:T(8,128)S(1)} %get-tuple-element.30.meta, s32[16]{0:T(128)S(1)} %compare_select_fusion.2.place, bf16[72,4096]{1,0:T(8,128)(2,1)S(1)} %collective-permute-done.4.far, ...), custom_call_target="tpu_custom_call" | custom-call | flops 603979776 | bytes 1179648 | tf_op jit(solution)/shard_map/late_tiles/pallas_call | solution.py:325
  21.9 1.9 %collective-permute-start.6 = (bf16[8,72,128]{2,1,0:T(8,128)(2,1)}, bf16[8,72,128]{2,1,0:T(8,128)(2,1)S(1)}, u32[]{:S(2)}, u32[]{:S(2)}) collective-permute-start(bf16[8,72,128]{2,1,0:T(8,128)(2,1)} %get-tuple-element.36), channel_id=1, source_target_pairs={{0,2},{1,3},{2,0},{3,1},{4,6},{5,7},{6,4},{7,5},{8,10},{9,11},{10,... | collective-permute-start | bytes 442376 | tf_op jit(solution)/shard_map/ppermute | solution.py:263
  23.8 0.1 collective-permute-start.7
  23.9 0.0 collective-permute-done.5.refs_4_
  23.9 4.9 %collective-permute-done.6.refs_5_ = bf16[8,72,128]{2,1,0:T(8,128)(2,1)S(1)} collective-permute-done((bf16[8,72,128]{2,1,0:T(8,128)(2,1)}, bf16[8,72,128]{2,1,0:T(8,128)(2,1)S(1)}, u32[]{:S(2)}, u32[]{:S(2)}) %collective-permute-start.6) | collective-permute-done | bytes 147488 | tf_op jit(solution)/shard_map/ppermute | solution.py:263
  28.8 2.6 %collective-permute-done.7.refs_6_ = bf16[8,72,128]{2,1,0:T(8,128)(2,1)S(1)} collective-permute-done((bf16[8,72,128]{2,1,0:T(8,128)(2,1)}, bf16[8,72,128]{2,1,0:T(8,128)(2,1)S(1)}, u32[]{:S(2)}, u32[]{:S(2)}) %collective-permute-start.7) | collective-permute-done | bytes 147488 | tf_op jit(solution)/shard_map/ppermute | solution.py:263
  31.3 0.8 %plane_sum.1 = (f32[4,72,128]{2,1,0:T(8,128)S(1)}, bf16[4,72,128]{2,1,0:T(8,128)(2,1)S(1)}, bf16[4,72,128]{2,1,0:T(8,128)(2,1)S(1)}, bf16[4,72,128]{2,1,0:T(8,128)(2,1)S(1)}) custom-call(s32[1]{0:T(128)} %bitcast.6.me, s32[8]{0:T(128)S(1)} %collective-permute-done.1.refs_0_, s32[8]{0:T(128)S(1)} %collective-permute-done.2.refs_1_, ...), custom_call_target="tpu_custom_call" | custom-call | tf_op jit(solution)/shard_map/plane_sum/pallas_call | solution.py:348
  32.2 6.8 %collective-permute-start.10 = (bf16[4,72,128]{2,1,0:T(8,128)(2,1)S(1)}, bf16[4,72,128]{2,1,0:T(8,128)(2,1)S(1)}, u32[]{:S(2)}, u32[]{:S(2)}) collective-permute-start(bf16[4,72,128]{2,1,0:T(8,128)(2,1)S(1)} %get-tuple-element.41), channel_id=1, source_target_pairs={{0,12},{1,13},{2,14},{3,15},{4,8},{5,9},{6,10},{7,11},{8,4},{9,5},... | collective-permute-start | bytes 221192 | tf_op jit(solution)/shard_map/ppermute | solution.py:263
  39.0 0.6 %collective-permute-start.9 = (bf16[4,72,128]{2,1,0:T(8,128)(2,1)S(1)}, bf16[4,72,128]{2,1,0:T(8,128)(2,1)S(1)}, u32[]{:S(2)}, u32[]{:S(2)}) collective-permute-start(bf16[4,72,128]{2,1,0:T(8,128)(2,1)S(1)} %get-tuple-element.40), channel_id=1, source_target_pairs={{0,8},{1,9},{2,10},{3,11},{4,12},{5,13},{6,14},{7,15},{8,0},{9,1},... | collective-permute-start | bytes 221192 | tf_op jit(solution)/shard_map/ppermute | solution.py:263
  39.6 0.1 fusion.choose
  39.7 2.3 %collective-permute-done.10.refs_3_ = bf16[4,72,128]{2,1,0:T(8,128)(2,1)S(1)} collective-permute-done((bf16[4,72,128]{2,1,0:T(8,128)(2,1)S(1)}, bf16[4,72,128]{2,1,0:T(8,128)(2,1)S(1)}, u32[]{:S(2)}, u32[]{:S(2)}) %collective-permute-start.10) | collective-permute-done | bytes 73760 | tf_op jit(solution)/shard_map/ppermute | solution.py:263
  42.0 2.4 %collective-permute-done.8.refs_1_ = bf16[4,72,128]{2,1,0:T(8,128)(2,1)S(1)} collective-permute-done((bf16[4,72,128]{2,1,0:T(8,128)(2,1)S(1)}, bf16[4,72,128]{2,1,0:T(8,128)(2,1)S(1)}, u32[]{:S(2)}, u32[]{:S(2)}) %collective-permute-start.8) | collective-permute-done | bytes 73760 | tf_op jit(solution)/shard_map/ppermute | solution.py:263
  44.4 1.4 %collective-permute-done.9.refs_2_ = bf16[4,72,128]{2,1,0:T(8,128)(2,1)S(1)} collective-permute-done((bf16[4,72,128]{2,1,0:T(8,128)(2,1)S(1)}, bf16[4,72,128]{2,1,0:T(8,128)(2,1)S(1)}, u32[]{:S(2)}, u32[]{:S(2)}) %collective-permute-start.9) | collective-permute-done | bytes 73760 | tf_op jit(solution)/shard_map/ppermute | solution.py:263
  45.8 1.3 %embed.1 = (bf16[4,72,128]{2,1,0:T(8,128)(2,1)}, bf16[32,1024]{1,0:T(8,128)(2,1)}) custom-call(bf16[128,128]{1,0:T(8,128)(2,1)S(1)} %fusion.choose, bf16[16,72,1024]{2,1,0:T(8,128)(2,1)S(1)} %bitcast.9, f32[1,1024]{1,0:T(1,128)S(1)} %bitcast.10, f32[4,72,128]{2,1,0:T(8,128)S(1)} %get-tuple-element.38.refs_0_, ...), custom_call_target="tpu_custom_call" | custom-call | tf_op jit(solution)/shard_map/embed/pallas_call | solution.py:364
  (12 shorter events, 0.1 us)
Async XLA Ops:
  0.6 8.0 %collective-permute-start = (bf16[72,8192]{1,0:T(8,128)(2,1)}, bf16[72,8192]{1,0:T(8,128)(2,1)S(1)}, u32[]{:S(2)}, u32[]{:S(2)}) collective-permute-start(bf16[72,8192]{1,0:T(8,128)(2,1)} %source.1), channel_id=1, source_target_pairs={{0,1},{1,0},{2,3},{3,2},{4,5},{5,4},{6,7},{7,6},{8,9},{9,8},{10,11... | collective-permute-start | bytes 3538952 | tf_op jit(solution)/shard_map/ppermute | solution.py:263
  2.3 16.8 %collective-permute-start.4 = (bf16[72,4096]{1,0:T(8,128)(2,1)S(1)}, bf16[72,4096]{1,0:T(8,128)(2,1)S(1)}, u32[]{:S(2)}, u32[]{:S(2)}) collective-permute-start(bf16[72,4096]{1,0:T(8,128)(2,1)S(1)} %constant_dynamic-slice_fusion), channel_id=1, source_target_pairs={{0,15},{1,2},{2,1},{3,4},{4,3},{5,6},{6,5},{7,8},{8,7},{9,10},{10,... | collective-permute-start | bytes 1769480 | tf_op jit(solution)/shard_map/ppermute | solution.py:266
  8.6 2.9 %copy-start.2 = (s32[16]{0:T(128)S(1)}, s32[16]{0:T(128)}, u32[]{:S(2)}) copy-start(s32[16]{0:T(128)} %param.13) | copy-start | bytes 196
  8.7 5.4 %copy-start.1 = (bf16[1152,1024]{1,0:T(8,128)(2,1)S(1)}, bf16[1152,1024]{1,0:T(8,128)(2,1)}, u32[]{:S(2)}) copy-start(bf16[1152,1024]{1,0:T(8,128)(2,1)} %param.14) | copy-start | bytes 7077892
  12.0 3.4 %collective-permute-start.1 = (s32[8]{0:T(128)S(1)}, s32[8]{0:T(128)S(1)}, u32[]{:S(2)}, u32[]{:S(2)}) collective-permute-start(s32[8]{0:T(128)S(1)} %get-tuple-element.49), channel_id=1, source_target_pairs={{0,1},{1,0},{2,3},{3,2},{4,5},{5,4},{6,7},{7,6},{8,9},{9,8},{10,11... | collective-permute-start | bytes 104 | tf_op jit(solution)/shard_map/ppermute | solution.py:263
  12.0 7.0 %collective-permute-start.2 = (s32[8]{0:T(128)S(1)}, s32[8]{0:T(128)S(1)}, u32[]{:S(2)}, u32[]{:S(2)}) collective-permute-start(s32[8]{0:T(128)S(1)} %get-tuple-element.48), channel_id=1, source_target_pairs={{0,2},{1,3},{2,0},{3,1},{4,6},{5,7},{6,4},{7,5},{8,10},{9,11},{10,... | collective-permute-start | bytes 104 | tf_op jit(solution)/shard_map/ppermute | solution.py:263
  14.1 5.0 %collective-permute-start.3 = (s32[8]{0:T(128)S(1)}, s32[8]{0:T(128)S(1)}, u32[]{:S(2)}, u32[]{:S(2)}) collective-permute-start(s32[8]{0:T(128)S(1)} %get-tuple-element.47), channel_id=1, source_target_pairs={{0,3},{1,2},{2,1},{3,0},{4,7},{5,6},{6,5},{7,4},{8,11},{9,10},{10,... | collective-permute-start | bytes 104 | tf_op jit(solution)/shard_map/ppermute | solution.py:263
  19.0 26.8 %copy-start = (f32[1024]{0:T(1024)S(1)}, f32[1024]{0:T(1024)}, u32[]{:S(2)}) copy-start(f32[1024]{0:T(1024)} %param.15) | copy-start | bytes 12292
  21.9 2.1 %collective-permute-start.5 = (bf16[8,72,128]{2,1,0:T(8,128)(2,1)}, bf16[8,72,128]{2,1,0:T(8,128)(2,1)S(1)}, u32[]{:S(2)}, u32[]{:S(2)}) collective-permute-start(bf16[8,72,128]{2,1,0:T(8,128)(2,1)} %get-tuple-element.35), channel_id=1, source_target_pairs={{0,1},{1,0},{2,3},{3,2},{4,5},{5,4},{6,7},{7,6},{8,9},{9,8},{10,11... | collective-permute-start | bytes 442376 | tf_op jit(solution)/shard_map/ppermute | solution.py:263
  21.9 6.9 %collective-permute-start.6 = (bf16[8,72,128]{2,1,0:T(8,128)(2,1)}, bf16[8,72,128]{2,1,0:T(8,128)(2,1)S(1)}, u32[]{:S(2)}, u32[]{:S(2)}) collective-permute-start(bf16[8,72,128]{2,1,0:T(8,128)(2,1)} %get-tuple-element.36), channel_id=1, source_target_pairs={{0,2},{1,3},{2,0},{3,1},{4,6},{5,7},{6,4},{7,5},{8,10},{9,11},{10,... | collective-permute-start | bytes 442376 | tf_op jit(solution)/shard_map/ppermute | solution.py:263
  23.8 7.5 %collective-permute-start.7 = (bf16[8,72,128]{2,1,0:T(8,128)(2,1)}, bf16[8,72,128]{2,1,0:T(8,128)(2,1)S(1)}, u32[]{:S(2)}, u32[]{:S(2)}) collective-permute-start(bf16[8,72,128]{2,1,0:T(8,128)(2,1)} %get-tuple-element.37), channel_id=1, source_target_pairs={{0,3},{1,2},{2,1},{3,0},{4,7},{5,6},{6,5},{7,4},{8,11},{9,10},{10,... | collective-permute-start | bytes 442376 | tf_op jit(solution)/shard_map/ppermute | solution.py:263
  32.2 9.8 %collective-permute-start.10 = (bf16[4,72,128]{2,1,0:T(8,128)(2,1)S(1)}, bf16[4,72,128]{2,1,0:T(8,128)(2,1)S(1)}, u32[]{:S(2)}, u32[]{:S(2)}) collective-permute-start(bf16[4,72,128]{2,1,0:T(8,128)(2,1)S(1)} %get-tuple-element.41), channel_id=1, source_target_pairs={{0,12},{1,13},{2,14},{3,15},{4,8},{5,9},{6,10},{7,11},{8,4},{9,5},... | collective-permute-start | bytes 221192 | tf_op jit(solution)/shard_map/ppermute | solution.py:263
  39.0 5.4 %collective-permute-start.8 = (bf16[4,72,128]{2,1,0:T(8,128)(2,1)S(1)}, bf16[4,72,128]{2,1,0:T(8,128)(2,1)S(1)}, u32[]{:S(2)}, u32[]{:S(2)}) collective-permute-start(bf16[4,72,128]{2,1,0:T(8,128)(2,1)S(1)} %get-tuple-element.39), channel_id=1, source_target_pairs={{0,4},{1,5},{2,6},{3,7},{4,0},{5,1},{6,2},{7,3},{8,12},{9,13},{10,... | collective-permute-start | bytes 221192 | tf_op jit(solution)/shard_map/ppermute | solution.py:263
  39.0 6.8 %collective-permute-start.9 = (bf16[4,72,128]{2,1,0:T(8,128)(2,1)S(1)}, bf16[4,72,128]{2,1,0:T(8,128)(2,1)S(1)}, u32[]{:S(2)}, u32[]{:S(2)}) collective-permute-start(bf16[4,72,128]{2,1,0:T(8,128)(2,1)S(1)} %get-tuple-element.40), channel_id=1, source_target_pairs={{0,8},{1,9},{2,10},{3,11},{4,12},{5,13},{6,14},{7,15},{8,0},{9,1},... | collective-permute-start | bytes 221192 | tf_op jit(solution)/shard_map/ppermute | solution.py:263
where the time goes:
time: 47 us; the launch traced here: 47.1 us
  starting transfers between devices  17.8 us (38%)
  waiting for transfers between devices  17.2 us (37%)
  Pallas kernels  7.83 us (17%)
  local copies, waits for them, and re-layouts  2.49 us (5%)
  between operations  1.39 us (3%)
    ppermute x10, waiting for transfers between devices, swap(): return lax.ppermute(x, 'dom', [(i, i ^ q) for i in range(peers)])  17.2 us
    ppermute x10, starting transfers between devices, swap(): return lax.ppermute(x, 'dom', [(i, i ^ q) for i in range(peers)])  12 us
    ppermute x1, starting transfers between devices, local(): lax.ppermute(lax.dynamic_slice_in_dim(source, core * width, width, axis=1...  5.73 us
    pallas_call x1, Pallas kernels, local(): pl.pallas_call(functools.partial(early_kernel, slots), out_shape=(pltpu.V...  2.88 us
    pallas_call x1, Pallas kernels, local(): pl.pallas_call(functools.partial(late_kernel, tiles, slots), out_shape=(o...  2.82 us
    reshape x1, local copies, waits for them, and re-layouts, local(): weight = embed_weight.reshape(channels, area, emb).transpose(1, 0, 2)  1.3 us
    pallas_call x1, Pallas kernels, local(): pl.pallas_call(final_kernel, out_shape=(jax.ShapeDtypeStruct(part, jnp.bf...  1.29 us
    dynamic_slice x1, local copies, waits for them, and re-layouts, local(): lax.dynamic_slice_in_dim(source, core * width, width, axis=1)  1.1 us
  transfers between devices with their start and end apart: 11, of which 6 were waited for; matrix products, arithmetic and copies ran while one was open for 6% of the time, Pallas kernels for 6%

commit v1 on v0

v1 whole, which is shorter than its diff:
```python
import functools

import jax
import jax.numpy as jnp
from jax import lax
from jax.experimental import pallas as pl
from jax.experimental.pallas import tpu as pltpu
from jax.sharding import PartitionSpec as P

PATCH = 4
CAP = 2
TB_DEV = 4
LANES = 128
SEG = 4
UNROLL = 8
CHUNK = 64
VMEM = pl.BlockSpec(memory_space=pltpu.VMEM)
SMEM = pl.BlockSpec(memory_space=pltpu.SMEM)
ANY = pl.BlockSpec(memory_space=pl.ANY)


def up(n, step):
    return -(-n // step) * step


def list_rows(tiles, slots):
    entries = up(up(tiles + slots * (SEG - 1), SEG * UNROLL), LANES) // LANES
    return entries, -(-entries // SEG)


def iota(shape, dim):
    return lax.broadcasted_iota(jnp.int32, shape, dim)


def ones_of(mask):
    return jnp.where(mask, 1.0, 0.0)


def dot(a, b, dims):
    return lax.dot_general(
        a.astype(jnp.bfloat16),
        b.astype(jnp.bfloat16),
        (dims, ((), ())),
        preferred_element_type=jnp.float32,
    )


def store_row(out, row, values):
    for r in range(values.shape[1] // LANES):
        out[row + r : row + r + 1, :] = values[:, r * LANES : (r + 1) * LANES]


def schedule(block, slot, kinds, slots, outs):
    tiles = block.shape[1]
    bits = tiles.bit_length()
    entries, segments = list_rows(tiles, slots)
    slot_is = slot == iota((slots, tiles), 0)
    chosen = [slot_is & kind for kind in kinds]
    before = ones_of(iota((tiles, tiles), 0) < iota((tiles, tiles), 1))
    ranks = dot(jnp.concatenate([ones_of(c) for c in chosen], axis=0), before, ((1,), (0,)))
    upto = ones_of(iota((slots, slots), 1) <= iota((slots, slots), 0))
    count = tiles - iota((1, tiles), 1)
    for k, (mask, out) in enumerate(zip(chosen, outs)):
        rank = ranks[k * slots : (k + 1) * slots]
        total = jnp.sum(ones_of(mask), axis=1, keepdims=True).astype(jnp.int32)
        length = jnp.broadcast_to((total + (SEG - 1)) // SEG, (slots, LANES))
        ends = dot(upto, length.astype(jnp.float32), ((1,), (0,))).astype(jnp.int32)
        begins = (ends - length)[:, :1].astype(jnp.float32)
        place = jnp.sum(jnp.where(mask, rank + begins * SEG + 1.0, 0.0), axis=0, keepdims=True)
        place = place.astype(jnp.int32) - 1
        at_row = (place >> 7) == iota((up(entries, 8), tiles), 0)
        at_lane = ones_of((place & (LANES - 1)) == iota((LANES, tiles), 0))

        def listed(value):
            rows = jnp.where(at_row, value.astype(jnp.float32), 0.0)
            return dot(rows, at_lane, ((1,), (1,)))[:entries].astype(jnp.int32)

        out[:entries, :] = (listed(block) << bits) | (listed(count >> 5) << 5) | listed(count & 31)
        passed = ones_of(ends[:, :1] <= iota((slots, segments * LANES), 1))
        owner = jnp.sum(passed, axis=0, keepdims=True).astype(jnp.int32)
        store_row(out, entries, jnp.minimum(owner, slots - 1))
        out[entries + segments : entries + segments + 1, :] = ends[slots - 1 : slots, :]


def slot_places(dest, me, members):
    slots = dest.shape[1]
    a, b = iota((slots, slots), 0), iota((slots, slots), 1)
    column = jnp.sum(jnp.where(a == b, dest.astype(jnp.float32), 0.0), axis=1, keepdims=True)
    column = column.astype(jnp.int32)
    owner = column // TB_DEV
    earlier = ones_of((owner == dest // TB_DEV) & (b < a))
    rank = jnp.sum(earlier, axis=1, keepdims=True).astype(jnp.int32)
    return owner & (members - 1), (owner // members) ^ (me // members), rank, column & (TB_DEV - 1)


def inverse(spot, valid, value, default, width):
    hit = valid & (spot == iota((spot.shape[0], up(width, LANES)), 1))
    found = jnp.sum(jnp.where(hit, (value - default).astype(jnp.float32), 0.0), axis=0, keepdims=True)
    return found.astype(jnp.int32) + default


def run_segments(tiles, slots, meta, x, w, acc):
    entries, segments = list_rows(tiles, slots)
    bits = tiles.bit_length()
    total = meta[entries + segments, 0]

    def step(i, carry):
        results = []
        for u in range(UNROLL):
            first = (i * UNROLL + u) * SEG
            row, lane = first >> 7, first & (LANES - 1)
            xs, ws = [], []
            for k in range(SEG):
                code = meta[row, lane + k]
                column = pl.multiple_of((code >> bits) * LANES, LANES)
                xs.append(x[:, pl.ds(column, LANES)])
                ws.append(w[tiles - (code & ((1 << bits) - 1))])
            results.append(
                jnp.dot(
                    jnp.concatenate(xs, axis=1),
                    jnp.concatenate(ws, axis=0),
                    preferred_element_type=jnp.float32,
                )
            )
        for u in range(UNROLL):
            g = i * UNROLL + u
            slot = meta[entries + (g >> 7), g & (LANES - 1)]
            acc[slot] += results[u]
        return carry

    lax.fori_loop(0, (total + UNROLL - 1) // UNROLL, step, 0)


def early_kernel(members, spans, me, count, *refs):
    n = len(spans)
    tile_source, tile_slot, dest, source, near, weights = refs[:6]
    peer_dests, refs = refs[6 : 5 + members], refs[5 + members :]
    acc, held, late_lists, spots, refs = refs[0], refs[1], refs[2 : 2 + n], refs[2 + n : 2 + 2 * n], refs[2 + 2 * n :]
    x, ids, lists, meta_a, meta_b, sems, weight_sems = refs
    tiles, slots = tile_source.shape[1], dest.shape[1]
    cells = source.shape[1]
    live, me, core = count[0], me[0], me[0] & 1
    chunks = tiles // CHUNK

    def copy(c):
        part = pl.ds(c * CHUNK, CHUNK)
        return pltpu.make_async_copy(weights.at[part], held.at[part], weight_sems.at[c])

    ids_in = [
        pltpu.make_async_copy(tile_source, ids.at[0], sems.at[0]),
        pltpu.make_async_copy(tile_slot, ids.at[1], sems.at[1]),
    ]
    for c in ids_in:
        c.start()
    for c in range(chunks):
        pl.when(c * CHUNK < live)(lambda c=c: copy(c).start())
    half = cells // 2
    first = pl.multiple_of(core * half, LANES)
    cells_in = [
        pltpu.make_async_copy(source, x.at[:, pl.ds(0, cells)], sems.at[2]),
        pltpu.make_async_copy(near.at[:, pl.ds(first, half)], x.at[:, pl.ds(cells, half)], sems.at[3]),
    ]
    for c in cells_in:
        c.start()
    for c in ids_in:
        c.wait()

    own = cells // LANES
    rim = own // 2
    place = ids[0]
    on_left, on_right = place < rim, place >= rim + own
    inner = ~(on_left | on_right)
    at_hand = inner | (on_left & (core == 1)) | (on_right & (core == 0))
    offset = jnp.where(on_right, place - own - rim, place)
    block = jnp.where(inner, place - rim, jnp.where(at_hand, own + offset, offset))
    tile_ids = iota((1, tiles), 1)
    alive = tile_ids < live
    member, plane, rank, block_row = slot_places(dest[...], me, members)
    member = member ^ (me & (members - 1))
    kinds = [alive & at_hand & (tile_ids < tiles // 2), alive & at_hand & (tile_ids >= tiles // 2)]
    kinds += [alive & ~at_hand & (plane >= lo) & (plane < hi) for lo, hi in spans]
    schedule(block, ids[1], kinds, slots, (lists.at[0], lists.at[1], *late_lists))
    to_scalars = [
        pltpu.make_async_copy(lists.at[0], meta_a, sems.at[4]),
        pltpu.make_async_copy(lists.at[1], meta_b, sems.at[5]),
    ]
    for c in to_scalars:
        c.start()

    entries, segments = list_rows(tiles, slots)
    peer_places = [slot_places(d[...], me, members) for d in peer_dests]
    for (lo, hi), late_list, spot in zip(spans, late_lists, spots):
        dense, rows = (hi - lo) * TB_DEV, (hi - lo) * CAP
        inside = (plane >= lo) & (plane < hi)
        goes = jnp.where(
            member == 0,
            (plane - lo) * TB_DEV + block_row,
            dense + (member - 1) * rows + (plane - lo) * CAP + rank,
        )
        width = dense + (members - 1) * rows
        slot_ids = iota((slots, 1), 0)
        store_row(late_list, entries + segments + 1, inverse(goes, inside, slot_ids, slots, width))
        total = None
        for q, (peer_member, peer_plane, peer_rank, peer_row) in enumerate(peer_places):
            inside = (peer_plane >= lo) & (peer_plane < hi) & (peer_member == (me & (members - 1)))
            comes = q * rows + (peer_plane - lo) * CAP + peer_rank
            value = (peer_plane - lo) * TB_DEV + peer_row
            found = inverse(comes, inside, value - dense, 0, (members - 1) * rows)
            total = found if total is None else total + found
        store_row(spot, 0, total + dense)

    acc[...] = jnp.zeros_like(acc)
    held[tiles] = jnp.zeros(held.shape[1:], held.dtype)
    for c in (*cells_in, *to_scalars):
        c.wait()
    for part, meta in ((0, meta_a), (1, meta_b)):
        for c in range(part * chunks // 2, (part + 1) * chunks // 2):
            pl.when(c * CHUNK < live)(lambda c=c: copy(c).wait())
        run_segments(tiles, slots, meta, x, held, acc)


def late_kernel(tiles, slots, meta, far, partial, held, *rest):
    *outs, acc = rest
    acc[:slots] = partial[...]
    acc[slots] = jnp.zeros(acc.shape[1:], acc.dtype)
    run_segments(tiles, slots, meta, far, held, acc)
    spot = sum(list_rows(tiles, slots)) + 1
    p = 0
    for out in outs:
        for r in range(out.shape[0]):
            out[r] = acc[meta[spot + p // LANES, p % LANES]].astype(out.dtype)
            p += 1


def plane_kernel(members, me, spots, own, *refs):
    rows, outs, total = refs[: members - 1], refs[members - 1 : -1], refs[-1]
    dense = own.shape[0]
    total[:dense] = own[...]
    p = 0
    for row in rows:
        for r in range(row.shape[0]):
            total[spots[p // LANES, p % LANES]] += row[r].astype(jnp.float32)
            p += 1
    if len(outs) == 1:
        planes = dense // TB_DEV
        for m in range(planes):
            at = pl.ds((me[0] ^ m) * TB_DEV, TB_DEV)
            outs[0][at] = total[m * TB_DEV : (m + 1) * TB_DEV].astype(outs[0].dtype)
    else:
        for m, out in enumerate(outs):
            out[...] = total[m * TB_DEV : (m + 1) * TB_DEV].astype(out.dtype)


def final_kernel(choose, weight, bias, *refs):
    *parts, remapped, embedded, turned = refs
    blocks, channels, cells = remapped.shape
    for b in range(blocks):
        value = sum(p[i + b].astype(jnp.float32) for p in parts for i in range(0, p.shape[0], blocks))
        value = value.astype(jnp.bfloat16)
        remapped[b] = value
        turned[b] = lax.dot_general(
            choose[...], value, (((1,), (1,)), ((), ())), preferred_element_type=jnp.float32
        )
    per_block = cells // (PATCH * PATCH)
    total = jnp.broadcast_to(bias[...], (blocks * per_block, bias.shape[1]))
    for s in range(PATCH * PATCH):
        rows = turned[:, s * per_block : (s + 1) * per_block, :]
        rows = rows.reshape(blocks * per_block, channels).astype(jnp.bfloat16)
        total = total + jnp.dot(rows, weight[s], preferred_element_type=jnp.float32)
    embedded[...] = total.astype(jnp.bfloat16)


def chooser(cells):
    per_block = cells // (PATCH * PATCH)
    row = jnp.arange(cells, dtype=jnp.int32)
    r, q, p = row // (PATCH * per_block), row // per_block % PATCH, row % per_block
    wanted = r * (PATCH * per_block) + p * PATCH + q
    return (wanted[:, None] == jnp.arange(cells, dtype=jnp.int32)[None, :]).astype(jnp.bfloat16)


def in_vmem(x):
    return pltpu.with_memory_space_constraint(x, pltpu.VMEM)


def in_hbm(x):
    return pltpu.with_memory_space_constraint(x, pltpu.HBM)


def limit(mib):
    return pltpu.CompilerParams(vmem_limit_bytes=mib << 20)


def local(
    source, tile_weight, tile_source, tile_slot, tile_count, dest_block, embed_weight, embed_bias
):
    channels, own_cells = source.shape
    tiles, block_size, _ = tile_weight.shape
    slots = dest_block.shape[0]
    peers = lax.axis_size("dom")
    me = lax.axis_index("dom").astype(jnp.int32)
    core = me & 1
    width = own_cells // 2
    emb = embed_weight.shape[1]
    members = 4 if peers == 16 else 2
    planes = peers // members

    def swap(x, q):
        return lax.ppermute(x, "dom", [(i, i ^ q) for i in range(peers)])

    near = swap(source, 1)
    far = lax.ppermute(
        lax.dynamic_slice_in_dim(source, core * width, width, axis=1),
        "dom",
        [(i, (i + (1 if i % 2 else -1)) % peers) for i in range(peers)],
    )

    peer_dests = [swap(dest_block, q)[None, :] for q in range(1, members)]

    by_swap = planes == 4
    spans = ((2, 4), (0, 2)) if by_swap else ((0, planes),)
    entries, segments = list_rows(tiles, slots)

    def table(rows):
        return jax.ShapeDtypeStruct((up(rows, 8), LANES), jnp.int32)

    def map_rows(lo, hi):
        return up((hi - lo) * (TB_DEV + (members - 1) * CAP), LANES) // LANES

    acc_shape = (slots, channels, block_size)
    list_table = table(entries + segments + 1)
    flops = tiles * channels * block_size * block_size
    partial, held, *tables = pl.pallas_call(
        functools.partial(early_kernel, members, spans),
        out_shape=(
            pltpu.VMEM(acc_shape, jnp.float32),
            pltpu.VMEM((tiles + 1, block_size, block_size), jnp.bfloat16),
            *[table(entries + segments + 1 + map_rows(*span)) for span in spans],
            *[table(map_rows(*span)) for span in spans],
        ),
        in_specs=[SMEM, SMEM, ANY, ANY, VMEM, ANY, ANY, ANY] + [VMEM] * (members - 1),
        out_specs=(VMEM,) * (2 + 2 * len(spans)),
        scratch_shapes=[
            pltpu.VMEM((channels, own_cells + width), jnp.bfloat16),
            pltpu.VMEM((2, 1, tiles), jnp.int32),
            pltpu.VMEM((2, *list_table.shape), jnp.int32),
            pltpu.SMEM(list_table.shape, jnp.int32),
            pltpu.SMEM(list_table.shape, jnp.int32),
            pltpu.SemaphoreType.DMA((6,)),
            pltpu.SemaphoreType.DMA((tiles // CHUNK,)),
        ],
        compiler_params=limit(16),
        cost_estimate=pl.CostEstimate(
            flops=2 * flops, bytes_accessed=tile_weight.size * 2, transcendentals=0
        ),
        name="early_tiles",
    )(
        me[None],
        tile_count,
        in_hbm(tile_source[None, :]),
        in_hbm(tile_slot[None, :]),
        dest_block[None, :],
        in_hbm(source),
        near,
        in_hbm(tile_weight),
        *peer_dests,
    )
    late_lists, spots = tables[: len(spans)], tables[len(spans) :]

    area = PATCH * PATCH
    partial, embed_weight = lax.optimization_barrier((partial, embed_weight))
    weight = embed_weight.reshape(channels, area, emb).transpose(1, 0, 2)
    far, weight = lax.optimization_barrier((far, weight))

    cells = (channels, block_size)
    part = (TB_DEV, *cells)
    own_rows = []
    for (lo, hi), late_list in zip(spans, late_lists):
        own_shape = pltpu.VMEM(((hi - lo) * TB_DEV, *cells), jnp.float32)
        row_shape = jax.ShapeDtypeStruct(((hi - lo) * CAP, *cells), jnp.bfloat16)
        own, *rows = pl.pallas_call(
            functools.partial(late_kernel, tiles, slots),
            out_shape=(own_shape,) + (row_shape,) * (members - 1),
            in_specs=[SMEM, VMEM, VMEM, VMEM],
            out_specs=(VMEM,) * members,
            scratch_shapes=[pltpu.VMEM((slots + 1, *cells), jnp.float32)],
            compiler_params=limit(16),
            cost_estimate=pl.CostEstimate(
                flops=flops, bytes_accessed=2 * channels * width, transcendentals=0
            ),
            name="late_tiles",
        )(late_list, far, in_vmem(partial), in_vmem(held))
        own_rows.append((own, [swap(r, q + 1) for q, r in enumerate(rows)]))

    parts = []
    for (lo, hi), spot, (own, rows) in zip(spans, spots, own_rows):
        if by_swap:
            part_shapes = [
                jax.ShapeDtypeStruct(part, jnp.bfloat16) if m else pltpu.VMEM(part, jnp.float32)
                for m in range(lo, hi)
            ]
        else:
            part_shapes = [jax.ShapeDtypeStruct(own.shape, jnp.bfloat16)]
        sums = pl.pallas_call(
            functools.partial(plane_kernel, members),
            out_shape=tuple(part_shapes),
            in_specs=[SMEM] * 2 + [VMEM] * members,
            out_specs=(VMEM,) * len(part_shapes),
            scratch_shapes=[pltpu.VMEM((own.shape[0] + 1, *cells), jnp.float32)],
            compiler_params=limit(24),
            name="plane_sum",
        )((me // members)[None], spot, in_vmem(own), *rows)
        if by_swap:
            parts += [swap(s, m * members) if m else s for m, s in zip(range(lo, hi), sums)]
        else:
            columns = [[z * members + i for z in range(planes)] for i in range(members)]
            parts.append(lax.all_to_all(sums[0], "dom", 0, 0, tiled=True, axis_index_groups=columns))

    per_block = block_size // area
    return pl.pallas_call(
        final_kernel,
        out_shape=(
            jax.ShapeDtypeStruct(part, jnp.bfloat16),
            jax.ShapeDtypeStruct((TB_DEV * per_block, emb), jnp.bfloat16),
        ),
        in_specs=[VMEM] * (3 + len(parts)),
        out_specs=(VMEM, VMEM),
        scratch_shapes=[pltpu.VMEM((TB_DEV, block_size, channels), jnp.float32)],
        compiler_params=limit(16),
        name="embed",
    )(chooser(block_size), weight, embed_bias.reshape(1, emb), *parts)


def solution(mesh):
    placed = (
        P(None, ("groups", "dom")),
        P("dom", None, None),
        P("dom"),
        P("dom"),
        P("dom"),
        P("dom"),
        P(),
        P(),
    )
    return jax.shard_map(
        local,
        mesh=mesh,
        in_specs=placed,
        out_specs=(P(("groups", "dom"), None, None), P(("groups", "dom"), None)),
        check_vma=False,
    )
```

time: 47 us -> 67.5 us (1.44)
  local copies, waits for them, and re-layouts: 2.49 us -> 16.5 us
  Pallas kernels: 7.83 us -> 18.9 us
  waiting for transfers between devices: 17.2 us -> 13.5 us
  starting transfers between devices: 17.8 us -> 17 us
    unnamed x6 -> x18, local copies, waits for them, and re-layouts: 0.02 us -> 14.1 us
    pallas_call x2 -> x3, Pallas kernels: 3.72 us -> 13.6 us  [the longest x1 11.9 us: local(): pl.pallas_call(functools.partial(early_kernel, members, spans), out_shape...]
    ppermute x10 -> x13, waiting for transfers between devices: 17.2 us -> 13.5 us  [swap(): return lax.ppermute(x, 'dom', [(i, i ^ q) for i in range(peers)])]
    pallas_call x1 -> x2, Pallas kernels: 2.82 us -> 4 us  [local(): pl.pallas_call(functools.partial(late_kernel, tiles, slots), out_shape=(o...]
    ppermute x10 -> x13, starting transfers between devices: 12 us -> 11.3 us  [swap(): return lax.ppermute(x, 'dom', [(i, i ^ q) for i in range(peers)])]
  transfers between devices with their start and end apart: 11 -> 14, of which waited for: 6 -> 3; matrix products, arithmetic and copies ran while one was open for 6% -> 4% of each run, Pallas kernels for 6% -> 23%
where the time goes in v1:
time: 67.5 us; the launch traced here: 67.4 us
  Pallas kernels  18.9 us (28%)
  starting transfers between devices  17 us (25%)
  local copies, waits for them, and re-layouts  16.5 us (24%)
  waiting for transfers between devices  13.5 us (20%)
  between operations  1.38 us (2%)
    unnamed x18, local copies, waits for them, and re-layouts  14.1 us
    ppermute x13, waiting for transfers between devices, swap(): return lax.ppermute(x, 'dom', [(i, i ^ q) for i in range(peers)])  13.5 us
    pallas_call x1, Pallas kernels, local(): pl.pallas_call(functools.partial(early_kernel, members, spans), out_shape...  11.9 us
    ppermute x13, starting transfers between devices, swap(): return lax.ppermute(x, 'dom', [(i, i ^ q) for i in range(peers)])  11.3 us
    ppermute x1, starting transfers between devices, local(): lax.ppermute(lax.dynamic_slice_in_dim(source, core * width, width, axis=1...  5.73 us
    pallas_call x2, Pallas kernels, local(): pl.pallas_call(functools.partial(late_kernel, tiles, slots), out_shape=(o...  4 us
    pallas_call x2, Pallas kernels, local(): pl.pallas_call(functools.partial(plane_kernel, members), out_shape=tuple(...  1.71 us
  transfers between devices with their start and end apart: 14, of which 3 were waited for; matrix products, arithmetic and copies ran while one was open for 4% of the time, Pallas kernels for 23%

profile of v1, /device:TPU:0, one launch (start us, length us, event | category | flops | bytes accessed | tf_op | source)
XLA Modules:
  0.0 67.4 jit_solution(4857134411630617805)
XLA Ops:
  0.6 0.5 collective-permute-start.1
  1.1 1.1 %constant_dynamic-slice_fusion = bf16[72,4096]{1,0:T(8,128)(2,1)S(1)} fusion(bf16[72,8192]{1,0:T(8,128)(2,1)} %refs_3_.1, s32[]{:T(128)S(6)} %select_n.47), kind=kLoop, calls=%fused_computation.19 | loop fusion | bytes 1179652 | tf_op jit(solution)/shard_map/dynamic_slice | solution.py:312
  2.3 5.7 %collective-permute-start = (bf16[72,4096]{1,0:T(8,128)(2,1)S(1)}, bf16[72,4096]{1,0:T(8,128)(2,1)S(1)}, u32[]{:S(2)}, u32[]{:S(2)}) collective-permute-start(bf16[72,4096]{1,0:T(8,128)(2,1)S(1)} %constant_dynamic-slice_fusion), channel_id=1, source_target_pairs={{0,15},{1,2},{2,1},{3,4},{4,3},{5,6},{6,5},{7,8},{8,7},{9,10},{10,... | collective-permute-start | bytes 1769480 | tf_op jit(solution)/shard_map/ppermute | solution.py:311
  8.0 0.0 collective-permute-start.2
  8.0 0.0 collective-permute-start.3
  8.0 1.9 %collective-permute-start.4 = (s32[16]{0:T(128)}, s32[16]{0:T(128)S(1)}, u32[]{:S(2)}, u32[]{:S(2)}) collective-permute-start(s32[16]{0:T(128)} %param.13), channel_id=1, source_target_pairs={{0,3},{1,2},{2,1},{3,0},{4,7},{5,6},{6,5},{7,4},{8,11},{9,10},{10,... | collective-permute-start | bytes 200 | tf_op jit(solution)/shard_map/ppermute | solution.py:308
  10.5 0.0 collective-permute-done.2
  10.5 8.5 %collective-permute-done.3 = s32[16]{0:T(128)S(1)} collective-permute-done((s32[16]{0:T(128)}, s32[16]{0:T(128)S(1)}, u32[]{:S(2)}, u32[]{:S(2)}) %collective-permute-start.3) | collective-permute-done | bytes 96 | tf_op jit(solution)/shard_map/ppermute | solution.py:308
  19.0 0.7 copy-done.5
  19.7 11.9 %early_tiles.1 = (f32[16,72,128]{2,1,0:T(8,128)S(1)}, bf16[513,128,128]{2,1,0:T(8,128)(2,1)S(1)}, s32[16,128]{1,0:T(8,128)S(1)}, s32[16,128]{1,0:T(8,128)S(1)}, ...) custom-call(s32[1]{0:T(128)} %bitcast.me, s32[1]{0:T(128)S(6)} %copy.13.count, s32[1,512]{1,0:T(1,128)} %bitcast.20, ...), custom_call_target="tpu_custom_call" | custom-call | flops 1207959552 | bytes 16777216 | tf_op jit(solution)/shard_map/early_tiles/pallas_call | solution.py:332
  31.6 1.3 %copy.12 = bf16[72,16,1024]{2,0,1:T(8,128)(2,1)S(1)} copy(bf16[72,16,1024]{2,1,0:T(8,128)(2,1)S(1)} %bitcast.19) | data formatting | bytes 4718592 | tf_op jit(solution)/shard_map/reshape | solution.py:371
  32.9 2.1 %late_tiles.2 = (f32[8,72,128]{2,1,0:T(8,128)S(1)}, bf16[4,72,128]{2,1,0:T(8,128)(2,1)}, bf16[4,72,128]{2,1,0:T(8,128)(2,1)S(1)}, bf16[4,72,128]{2,1,0:T(8,128)(2,1)S(1)}) custom-call(s32[16,128]{1,0:T(8,128)S(1)} %get-tuple-element.28.meta, bf16[72,4096]{1,0:T(8,128)(2,1)S(1)} %collective-permute-done.far, f32[16,72,128]{2,1,0:T(8,128)S(1)} %get-tuple-element.30.partial, ...), custom_call_target="tpu_custom_call" | custom-call | flops 603979776 | bytes 589824 | tf_op jit(solution)/shard_map/late_tiles/pallas_call | solution.py:380
  35.0 5.7 %copy-done = bf16[513,128,128]{2,1,0:T(8,128)(2,1)} copy-done((bf16[513,128,128]{2,1,0:T(8,128)(2,1)}, bf16[513,128,128]{2,1,0:T(8,128)(2,1)S(1)}, u32[]{:S(2)}) %copy-start) | copy-done | bytes 16810008
  40.8 0.7 %copy-done.2 = f32[8,72,128]{2,1,0:T(8,128)} copy-done((f32[8,72,128]{2,1,0:T(8,128)}, f32[8,72,128]{2,1,0:T(8,128)S(1)}, u32[]{:S(2)}) %copy-start.2) | copy-done | bytes 294936
  41.5 0.6 copy-done.6
  42.1 0.6 copy-done.7
  42.8 2.2 %collective-permute-start.6 = (bf16[4,72,128]{2,1,0:T(8,128)(2,1)}, bf16[4,72,128]{2,1,0:T(8,128)(2,1)S(1)}, u32[]{:S(2)}, u32[]{:S(2)}) collective-permute-start(bf16[4,72,128]{2,1,0:T(8,128)(2,1)} %copy-done.7), channel_id=1, source_target_pairs={{0,2},{1,3},{2,0},{3,1},{4,6},{5,7},{6,4},{7,5},{8,10},{9,11},{10,... | collective-permute-start | bytes 221192 | tf_op jit(solution)/shard_map/ppermute | solution.py:308
  45.0 0.1 collective-permute-start.7
  45.1 5.8 %copy-done.1 = bf16[513,128,128]{2,1,0:T(8,128)(2,1)S(1)} copy-done((bf16[513,128,128]{2,1,0:T(8,128)(2,1)S(1)}, bf16[513,128,128]{2,1,0:T(8,128)(2,1)}, u32[]{:S(2)}) %copy-start.1) | copy-done | bytes 16810008
  50.9 1.9 %late_tiles.3 = (f32[8,72,128]{2,1,0:T(8,128)S(1)}, bf16[4,72,128]{2,1,0:T(8,128)(2,1)S(1)}, bf16[4,72,128]{2,1,0:T(8,128)(2,1)S(1)}, bf16[4,72,128]{2,1,0:T(8,128)(2,1)S(1)}) custom-call(s32[16,128]{1,0:T(8,128)S(1)} %get-tuple-element.39.meta, bf16[72,4096]{1,0:T(8,128)(2,1)S(1)} %collective-permute-done.far, ...), custom_call_target="tpu_custom_call" | custom-call | flops 603979776 | bytes 589824 | tf_op jit(solution)/shard_map/late_tiles/pallas_call | solution.py:380
  52.8 0.2 collective-permute-start.10
  53.0 1.7 %collective-permute-start.11 = (bf16[4,72,128]{2,1,0:T(8,128)(2,1)S(1)}, bf16[4,72,128]{2,1,0:T(8,128)(2,1)S(1)}, u32[]{:S(2)}, u32[]{:S(2)}) collective-permute-start(bf16[4,72,128]{2,1,0:T(8,128)(2,1)S(1)} %get-tuple-element.42), channel_id=1, source_target_pairs={{0,2},{1,3},{2,0},{3,1},{4,6},{5,7},{6,4},{7,5},{8,10},{9,11},{10,... | collective-permute-start | bytes 221192 | tf_op jit(solution)/shard_map/ppermute | solution.py:308
  54.7 0.1 collective-permute-start.12
  54.8 1.0 %plane_sum.2 = (bf16[4,72,128]{2,1,0:T(8,128)(2,1)S(1)}, bf16[4,72,128]{2,1,0:T(8,128)(2,1)S(1)}) custom-call(s32[1]{0:T(128)} %bitcast.10.me, s32[8,128]{1,0:T(8,128)S(1)} %get-tuple-element.27.spots, f32[8,72,128]{2,1,0:T(8,128)S(1)} %copy-done.3, bf16[4,72,128]{2,1,0:T(8,128)(2,1)} %collective-permute-done.5.refs_0_, ...), custom_call_target="tpu_custom_call" | custom-call | tf_op jit(solution)/shard_map/plane_sum/pallas_call | solution.py:403
  55.8 2.5 %collective-permute-start.8 = (bf16[4,72,128]{2,1,0:T(8,128)(2,1)S(1)}, bf16[4,72,128]{2,1,0:T(8,128)(2,1)S(1)}, u32[]{:S(2)}, u32[]{:S(2)}) collective-permute-start(bf16[4,72,128]{2,1,0:T(8,128)(2,1)S(1)} %get-tuple-element.36), channel_id=1, source_target_pairs={{0,8},{1,9},{2,10},{3,11},{4,12},{5,13},{6,14},{7,15},{8,0},{9,1},... | collective-permute-start | bytes 221192 | tf_op jit(solution)/shard_map/ppermute | solution.py:308
  58.2 1.1 %collective-permute-start.9 = (bf16[4,72,128]{2,1,0:T(8,128)(2,1)S(1)}, bf16[4,72,128]{2,1,0:T(8,128)(2,1)S(1)}, u32[]{:S(2)}, u32[]{:S(2)}) collective-permute-start(bf16[4,72,128]{2,1,0:T(8,128)(2,1)S(1)} %get-tuple-element.37), channel_id=1, source_target_pairs={{0,12},{1,13},{2,14},{3,15},{4,8},{5,9},{6,10},{7,11},{8,4},{9,5},... | collective-permute-start | bytes 221192 | tf_op jit(solution)/shard_map/ppermute | solution.py:308
  59.3 0.7 %plane_sum.3 = (f32[4,72,128]{2,1,0:T(8,128)S(1)}, bf16[4,72,128]{2,1,0:T(8,128)(2,1)S(1)}) custom-call(s32[1]{0:T(128)} %bitcast.10.me, s32[8,128]{1,0:T(8,128)S(1)} %get-tuple-element.38.spots, f32[8,72,128]{2,1,0:T(8,128)S(1)} %get-tuple-element.40.own, bf16[4,72,128]{2,1,0:T(8,128)(2,1)S(1)} %collective-permute-done.10.refs_0_, ...), custom_call_target="tpu_custom_call" | custom-call | tf_op jit(solution)/shard_map/plane_sum/pallas_call | solution.py:403
  60.1 1.0 %collective-permute-start.13 = (bf16[4,72,128]{2,1,0:T(8,128)(2,1)S(1)}, bf16[4,72,128]{2,1,0:T(8,128)(2,1)S(1)}, u32[]{:S(2)}, u32[]{:S(2)}) collective-permute-start(bf16[4,72,128]{2,1,0:T(8,128)(2,1)S(1)} %get-tuple-element.45), channel_id=1, source_target_pairs={{0,4},{1,5},{2,6},{3,7},{4,0},{5,1},{6,2},{7,3},{8,12},{9,13},{10,... | collective-permute-start | bytes 221192 | tf_op jit(solution)/shard_map/ppermute | solution.py:308
  61.1 0.1 fusion.choose
  61.1 3.8 %collective-permute-done.8.refs_0_ = bf16[4,72,128]{2,1,0:T(8,128)(2,1)S(1)} collective-permute-done((bf16[4,72,128]{2,1,0:T(8,128)(2,1)S(1)}, bf16[4,72,128]{2,1,0:T(8,128)(2,1)S(1)}, u32[]{:S(2)}, u32[]{:S(2)}) %collective-permute-start.8) | collective-permute-done | bytes 73760 | tf_op jit(solution)/shard_map/ppermute | solution.py:308
  65.0 1.2 %collective-permute-done.13.refs_3_ = bf16[4,72,128]{2,1,0:T(8,128)(2,1)S(1)} collective-permute-done((bf16[4,72,128]{2,1,0:T(8,128)(2,1)S(1)}, bf16[4,72,128]{2,1,0:T(8,128)(2,1)S(1)}, u32[]{:S(2)}, u32[]{:S(2)}) %collective-permute-start.13) | collective-permute-done | bytes 73760 | tf_op jit(solution)/shard_map/ppermute | solution.py:308
  66.1 1.3 %embed.1 = (bf16[4,72,128]{2,1,0:T(8,128)(2,1)}, bf16[32,1024]{1,0:T(8,128)(2,1)}) custom-call(bf16[128,128]{1,0:T(8,128)(2,1)S(1)} %fusion.choose, bf16[16,72,1024]{2,1,0:T(8,128)(2,1)S(1)} %bitcast.13, f32[1,1024]{1,0:T(1,128)S(1)} %bitcast.14, bf16[4,72,128]{2,1,0:T(8,128)(2,1)S(1)} %collective-permute-done.8.refs_0_, ...), custom_call_target="tpu_custom_call" | custom-call | tf_op jit(solution)/shard_map/embed/pallas_call | solution.py:419
  (24 shorter events, 0.1 us)
Async XLA Ops:
  0.6 18.4 %collective-permute-start.1 = (bf16[72,8192]{1,0:T(8,128)(2,1)}, bf16[72,8192]{1,0:T(8,128)(2,1)S(1)}, u32[]{:S(2)}, u32[]{:S(2)}) collective-permute-start(bf16[72,8192]{1,0:T(8,128)(2,1)} %refs_3_.1), channel_id=1, source_target_pairs={{0,1},{1,0},{2,3},{3,2},{4,5},{5,4},{6,7},{7,6},{8,9},{9,8},{10,11... | collective-permute-start | bytes 3538952 | tf_op jit(solution)/shard_map/ppermute | solution.py:308
  2.3 30.7 %collective-permute-start = (bf16[72,4096]{1,0:T(8,128)(2,1)S(1)}, bf16[72,4096]{1,0:T(8,128)(2,1)S(1)}, u32[]{:S(2)}, u32[]{:S(2)}) collective-permute-start(bf16[72,4096]{1,0:T(8,128)(2,1)S(1)} %constant_dynamic-slice_fusion), channel_id=1, source_target_pairs={{0,15},{1,2},{2,1},{3,4},{4,3},{5,6},{6,5},{7,8},{8,7},{9,10},{10,... | collective-permute-start | bytes 1769480 | tf_op jit(solution)/shard_map/ppermute | solution.py:311
  8.0 2.5 %collective-permute-start.2 = (s32[16]{0:T(128)}, s32[16]{0:T(128)S(1)}, u32[]{:S(2)}, u32[]{:S(2)}) collective-permute-start(s32[16]{0:T(128)} %param.13), channel_id=1, source_target_pairs={{0,1},{1,0},{2,3},{3,2},{4,5},{5,4},{6,7},{7,6},{8,9},{9,8},{10,11... | collective-permute-start | bytes 200 | tf_op jit(solution)/shard_map/ppermute | solution.py:308
  8.0 11.0 %collective-permute-start.3 = (s32[16]{0:T(128)}, s32[16]{0:T(128)S(1)}, u32[]{:S(2)}, u32[]{:S(2)}) collective-permute-start(s32[16]{0:T(128)} %param.13), channel_id=1, source_target_pairs={{0,2},{1,3},{2,0},{3,1},{4,6},{5,7},{6,4},{7,5},{8,10},{9,11},{10,... | collective-permute-start | bytes 200 | tf_op jit(solution)/shard_map/ppermute | solution.py:308
  8.0 11.0 %collective-permute-start.4 = (s32[16]{0:T(128)}, s32[16]{0:T(128)S(1)}, u32[]{:S(2)}, u32[]{:S(2)}) collective-permute-start(s32[16]{0:T(128)} %param.13), channel_id=1, source_target_pairs={{0,3},{1,2},{2,1},{3,0},{4,7},{5,6},{6,5},{7,4},{8,11},{9,10},{10,... | collective-permute-start | bytes 200 | tf_op jit(solution)/shard_map/ppermute | solution.py:308
  19.0 0.7 copy-start.5
  19.7 11.9 %copy-start.8 = (bf16[1152,1024]{1,0:T(8,128)(2,1)S(1)}, bf16[1152,1024]{1,0:T(8,128)(2,1)}, u32[]{:S(2)}) copy-start(bf16[1152,1024]{1,0:T(8,128)(2,1)} %param.14) | copy-start | bytes 7077892
  35.0 5.7 %copy-start = (bf16[513,128,128]{2,1,0:T(8,128)(2,1)}, bf16[513,128,128]{2,1,0:T(8,128)(2,1)S(1)}, u32[]{:S(2)}) copy-start(bf16[513,128,128]{2,1,0:T(8,128)(2,1)S(1)} %get-tuple-element.31.held) | copy-start | bytes 50429956
  40.8 0.7 %copy-start.2 = (f32[8,72,128]{2,1,0:T(8,128)}, f32[8,72,128]{2,1,0:T(8,128)S(1)}, u32[]{:S(2)}) copy-start(f32[8,72,128]{2,1,0:T(8,128)S(1)} %get-tuple-element.32.own) | copy-start | bytes 884740
  41.5 0.6 copy-start.6
  42.1 0.6 copy-start.7
  42.8 11.9 %collective-permute-start.5 = (bf16[4,72,128]{2,1,0:T(8,128)(2,1)}, bf16[4,72,128]{2,1,0:T(8,128)(2,1)}, u32[]{:S(2)}, u32[]{:S(2)}) collective-permute-start(bf16[4,72,128]{2,1,0:T(8,128)(2,1)} %get-tuple-element.33), channel_id=1, source_target_pairs={{0,1},{1,0},{2,3},{3,2},{4,5},{5,4},{6,7},{7,6},{8,9},{9,8},{10,11... | collective-permute-start | bytes 221192 | tf_op jit(solution)/shard_map/ppermute | solution.py:308
  42.8 12.0 %collective-permute-start.6 = (bf16[4,72,128]{2,1,0:T(8,128)(2,1)}, bf16[4,72,128]{2,1,0:T(8,128)(2,1)S(1)}, u32[]{:S(2)}, u32[]{:S(2)}) collective-permute-start(bf16[4,72,128]{2,1,0:T(8,128)(2,1)} %copy-done.7), channel_id=1, source_target_pairs={{0,2},{1,3},{2,0},{3,1},{4,6},{5,7},{6,4},{7,5},{8,10},{9,11},{10,... | collective-permute-start | bytes 221192 | tf_op jit(solution)/shard_map/ppermute | solution.py:308
  45.0 9.8 %collective-permute-start.7 = (bf16[4,72,128]{2,1,0:T(8,128)(2,1)}, bf16[4,72,128]{2,1,0:T(8,128)(2,1)S(1)}, u32[]{:S(2)}, u32[]{:S(2)}) collective-permute-start(bf16[4,72,128]{2,1,0:T(8,128)(2,1)} %copy-done.6), channel_id=1, source_target_pairs={{0,3},{1,2},{2,1},{3,0},{4,7},{5,6},{6,5},{7,4},{8,11},{9,10},{10,... | collective-permute-start | bytes 221192 | tf_op jit(solution)/shard_map/ppermute | solution.py:308
  45.1 5.8 %copy-start.1 = (bf16[513,128,128]{2,1,0:T(8,128)(2,1)S(1)}, bf16[513,128,128]{2,1,0:T(8,128)(2,1)}, u32[]{:S(2)}) copy-start(bf16[513,128,128]{2,1,0:T(8,128)(2,1)} %copy-done) | copy-start | bytes 50429956
  50.9 3.8 %copy-start.3 = (f32[8,72,128]{2,1,0:T(8,128)S(1)}, f32[8,72,128]{2,1,0:T(8,128)}, u32[]{:S(2)}) copy-start(f32[8,72,128]{2,1,0:T(8,128)} %copy-done.2) | copy-start | bytes 884740
  50.9 15.2 %copy-start.4 = (f32[1024]{0:T(1024)S(1)}, f32[1024]{0:T(1024)}, u32[]{:S(2)}) copy-start(f32[1024]{0:T(1024)} %param.15) | copy-start | bytes 12292
  52.8 6.5 %collective-permute-start.10 = (bf16[4,72,128]{2,1,0:T(8,128)(2,1)S(1)}, bf16[4,72,128]{2,1,0:T(8,128)(2,1)S(1)}, u32[]{:S(2)}, u32[]{:S(2)}) collective-permute-start(bf16[4,72,128]{2,1,0:T(8,128)(2,1)S(1)} %get-tuple-element.41), channel_id=1, source_target_pairs={{0,1},{1,0},{2,3},{3,2},{4,5},{5,4},{6,7},{7,6},{8,9},{9,8},{10,11... | collective-permute-start | bytes 221192 | tf_op jit(solution)/shard_map/ppermute | solution.py:308
  53.0 6.4 %collective-permute-start.11 = (bf16[4,72,128]{2,1,0:T(8,128)(2,1)S(1)}, bf16[4,72,128]{2,1,0:T(8,128)(2,1)S(1)}, u32[]{:S(2)}, u32[]{:S(2)}) collective-permute-start(bf16[4,72,128]{2,1,0:T(8,128)(2,1)S(1)} %get-tuple-element.42), channel_id=1, source_target_pairs={{0,2},{1,3},{2,0},{3,1},{4,6},{5,7},{6,4},{7,5},{8,10},{9,11},{10,... | collective-permute-start | bytes 221192 | tf_op jit(solution)/shard_map/ppermute | solution.py:308
  54.7 4.7 %collective-permute-start.12 = (bf16[4,72,128]{2,1,0:T(8,128)(2,1)S(1)}, bf16[4,72,128]{2,1,0:T(8,128)(2,1)S(1)}, u32[]{:S(2)}, u32[]{:S(2)}) collective-permute-start(bf16[4,72,128]{2,1,0:T(8,128)(2,1)S(1)} %get-tuple-element.43), channel_id=1, source_target_pairs={{0,3},{1,2},{2,1},{3,0},{4,7},{5,6},{6,5},{7,4},{8,11},{9,10},{10,... | collective-permute-start | bytes 221192 | tf_op jit(solution)/shard_map/ppermute | solution.py:308
  55.8 9.2 %collective-permute-start.8 = (bf16[4,72,128]{2,1,0:T(8,128)(2,1)S(1)}, bf16[4,72,128]{2,1,0:T(8,128)(2,1)S(1)}, u32[]{:S(2)}, u32[]{:S(2)}) collective-permute-start(bf16[4,72,128]{2,1,0:T(8,128)(2,1)S(1)} %get-tuple-element.36), channel_id=1, source_target_pairs={{0,8},{1,9},{2,10},{3,11},{4,12},{5,13},{6,14},{7,15},{8,0},{9,1},... | collective-permute-start | bytes 221192 | tf_op jit(solution)/shard_map/ppermute | solution.py:308
  58.2 6.7 %collective-permute-start.9 = (bf16[4,72,128]{2,1,0:T(8,128)(2,1)S(1)}, bf16[4,72,128]{2,1,0:T(8,128)(2,1)S(1)}, u32[]{:S(2)}, u32[]{:S(2)}) collective-permute-start(bf16[4,72,128]{2,1,0:T(8,128)(2,1)S(1)} %get-tuple-element.37), channel_id=1, source_target_pairs={{0,12},{1,13},{2,14},{3,15},{4,8},{5,9},{6,10},{7,11},{8,4},{9,5},... | collective-permute-start | bytes 221192 | tf_op jit(solution)/shard_map/ppermute | solution.py:308
  60.1 6.1 %collective-permute-start.13 = (bf16[4,72,128]{2,1,0:T(8,128)(2,1)S(1)}, bf16[4,72,128]{2,1,0:T(8,128)(2,1)S(1)}, u32[]{:S(2)}, u32[]{:S(2)}) collective-permute-start(bf16[4,72,128]{2,1,0:T(8,128)(2,1)S(1)} %get-tuple-element.45), channel_id=1, source_target_pairs={{0,4},{1,5},{2,6},{3,7},{4,0},{5,1},{6,2},{7,3},{8,12},{9,13},{10,... | collective-permute-start | bytes 221192 | tf_op jit(solution)/shard_map/ppermute | solution.py:308
